TPU v7x, 256 devices: a whole 4x4x8 slice. The times are simulated.
256 devices in a mesh: rep: 32 (over z_lo, x, core), tp: 8 (over z_hi, y).
Axes of the slice: x: 4, y: 4, z: 8 (z_hi: 2, z_lo: 4; z = z_hi * 4 + z_lo), core: 2. Of those that a mesh axis runs over, the one named last changes fastest.
Arguments:
- tokens_in: bfloat16 [32768, 8192], P('rep', 'tp'), may hold values from -1300 to 1300
- gain: float32 [8192], P('tp'), may hold values from 0.1 to 1.9
- cotangent: bfloat16 [32768, 1024], P('rep', 'tp'), may hold values from -12 to 12
- local_weight: bfloat16 [32, 8192, 1024], P('rep', 'tp'), may hold values from -6 to 1030
- packed_codes: int32 [32, 8192, 512], P('rep', 'tp'), may hold values from 0 to 255
- code_scales: float32 [32, 8192, 8], P('rep', 'tp'), may hold values from 0.02 to 1
- global_weight: float32 [8, 1024, 1024], P('tp', 'rep'), may hold values from -6 to 6
- momentum: float32 [8, 1024, 1024], P('tp', 'rep'), may hold values from -3 to 3
Outputs:
- projected: bfloat16 [32768, 1024], P('rep', 'tp')
- grad_x: bfloat16 [32768, 8192], P('rep', 'tp')
- new_local: bfloat16 [32, 8192, 1024], P('rep', 'tp')
- new_global: float32 [8, 1024, 1024], P('tp', 'rep')
- new_momentum: float32 [8, 1024, 1024], P('tp', 'rep')
All inputs are finite; a program needn't handle non-finite values.
Results may differ from a plain program's by a relative error of at most 0.017.
Values may be sent and summed in bfloat16 or wider, within the bound.
A program may use at most 64 MiB of HBM per device.

v0:
```python
import math

import jax
import jax.numpy as jnp
from jax import lax
from jax.sharding import PartitionSpec as P

D = 8192


epsilon = 1e-05
outer_rate = 0.7
outer_push = 0.9
keep_share = 0.5
inner_rate = 0.5


def decode(words, scales):
    planes = [jnp.bitwise_and(jnp.right_shift(words, 4 * plane), 15) - 8 for plane in range(2)]
    codes = jnp.concatenate(planes, axis=-1).astype(jnp.float32)
    layout = codes.shape
    grouped = codes.reshape(layout[:-1] + (layout[-1] // 128, 128)) * scales[..., None]
    return grouped.reshape(layout)


def local(
    tokens_in, gain, cotangent, local_weight, packed_codes, code_scales, global_weight, momentum
):
    factor = 1.0 / math.sqrt(D)
    weight = local_weight[0]
    wide = tokens_in.astype(jnp.float32)
    squares = lax.psum(jnp.sum(wide * wide, axis=-1), "tp")
    inverse = lax.rsqrt(squares / D + epsilon)[:, None]
    normed = (wide * inverse * gain).astype(jnp.bfloat16)
    partial_value = jnp.dot(normed, weight, preferred_element_type=jnp.float32) * factor
    partial_value = lax.optimization_barrier(partial_value.astype(jnp.bfloat16)).astype(jnp.float32)
    projected = lax.psum_scatter(
        partial_value.astype(jnp.bfloat16), "tp", scatter_dimension=1, tiled=True
    )
    piece = lax.all_gather(cotangent, "tp", axis=1, tiled=True)
    block = (
        lax.dot_general(normed, piece, (((0,), (0,)), ((), ())), preferred_element_type=jnp.float32)
        * factor
    )
    grad_normed = (
        lax.dot_general(piece, weight, (((1,), (1,)), ((), ())), preferred_element_type=jnp.float32)
        * factor
    )
    grad_weight, grad_normed = (block, grad_normed)
    scaled = gain * grad_normed
    inner = lax.psum(jnp.sum(scaled * wide, axis=-1), "tp")[:, None]
    grad_x = (inverse * scaled - wide * inverse**3 * inner / D).astype(jnp.bfloat16)
    words = packed_codes[0]
    scales = code_scales[0]
    summed = lax.psum_scatter(
        decode(words, scales).astype(jnp.bfloat16), "rep", scatter_dimension=0, tiled=True
    ).astype(jnp.float32)
    delta = summed / lax.axis_size("rep")
    new_momentum = outer_push * momentum[0] + delta
    new_global = global_weight[0] - outer_rate * (delta + outer_push * new_momentum)
    shared = new_global.astype(jnp.bfloat16)
    own_rows = weight.astype(jnp.float32)
    mixed = (
        keep_share * own_rows
        + (1.0 - keep_share) * lax.all_gather(shared, "rep", axis=0, tiled=True).astype(jnp.float32)
        - inner_rate * grad_weight
    )
    new_local = mixed.astype(jnp.bfloat16)
    return (projected, grad_x, new_local[None], new_global[None], new_momentum[None])


def solution(mesh):
    return jax.shard_map(
        local,
        mesh=mesh,
        in_specs=(
            P("rep", "tp"),
            P("tp"),
            P("rep", "tp"),
            P("rep", "tp", None),
            P("rep", "tp", None),
            P("rep", "tp", None),
            P("tp", "rep", None),
            P("tp", "rep", None),
        ),
        out_specs=(
            P("rep", "tp"),
            P("rep", "tp"),
            P("rep", "tp", None),
            P("tp", "rep", None),
            P("tp", "rep", None),
        ),
        check_vma=False,
    )
```

profile of v0, /device:TPU:1, one launch (start us, length us, event | category | flops | bytes accessed | tf_op | source)
XLA Modules:
  0.0 364.6 jit_solution(16400250277226878912)
XLA Ops:
  8.0 0.0 all-gather.3.cloned.1.call-start
  8.0 0.7 all-gather.3.cloned.1.call-update
  8.7 0.0 reduce-scatter.5.cloned.1.call-start
  8.8 1.0 copy.17
  9.7 3.5 and_add_fusion.1
  13.3 2.9 sub.21
  16.2 1.7 sub.23
  17.9 4.2 %fusion.9 = bf16[1024,8,128]{2,1,0:T(8,128)(2,1)S(1)} fusion(s32[1024,4,128]{2,1,0:T(4,128)} %sub.23, s32[1024,4,128]{2,1,0:T(4,128)} %sub.21, f32[1024,8]{1,0:T(8,128)S(1)} %copy.17), kind=kLoop, calls=%fused_computation.14 | loop fusion | flops 4194304 | bytes 6324224 | tf_op jit(solution)/shard_map/convert_element_type | solution.py:56
  22.1 2.0 copy.23
  24.1 0.0 reduce-scatter.5.cloned.1.call-update
  24.1 0.0 copy-start.2
  24.1 0.0 reduce-scatter.7.cloned.1.call-start
  24.2 2.9 copy.16
  27.0 0.0 copy-done.2
  27.0 57.5 %all-gather.3.cloned.1.call-done = bf16[1024,1024]{1,0:T(8,128)(2,1)} async-done(((bf16[1024,128]{1,0:T(8,128)(2,1)}), bf16[1024,1024]{1,0:T(8,128)(2,1)}) %all-gather.3.cloned.1.call-update) | async-done | bytes 2097168 | tf_op jit(solution)/shard_map/all_gather | solution.py:40
  84.6 6.6 %fusion.7 = (f32[1024]{0:T(1024)S(1)}, f32[1024]{0:T(1024)S(1)}, f32[1024,1024]{0,1:T(8,128)}) fusion(bf16[1024,1024]{0,1:T(8,128)(2,1)S(1)} %copy.16, f32[1024]{0:T(1024)S(1)} %broadcast_multiply_fusion, bf16[1024,1024]{1,0:T(8,128)(2,1)} %all-gather.3.cloned.1.call-done, bf16[1,1024,1024]{2,1,0:T(8,128)(2,1)} %param.11), kind=kOutput, calls=%fused_computation.11 | convolution fusion | flops 2153773056 | bytes 10498048 | tf_op jit(solution)/shard_map/dot_general | solution.py:46
  91.2 22.8 %all-reduce = (f32[1024]{0:T(1024)S(1)}, f32[1024]{0:T(1024)S(1)}) all-reduce(f32[1024]{0:T(1024)S(1)} %get-tuple-element.16, f32[1024]{0:T(1024)S(1)} %get-tuple-element.15), channel_id=1, replica_groups=mesh['rep'=32,'tp'=8] {'tp'}, use_global_device_ids=true, to_apply=%region_1.0 | all-reduce | flops 2048 | bytes 16384 | tf_op jit(solution)/shard_map/psum | solution.py:32
  114.0 5.5 %multiply_convert_fusion = bf16[1024,1024]{1,0:T(8,128)(2,1)} fusion(bf16[1,1024,1024]{2,1,0:T(8,128)(2,1)} %param.11, bf16[1024,1024]{0,1:T(8,128)(2,1)S(1)} %copy.16, f32[1024]{0:T(1024)S(1)} %copy-done.2, f32[1024]{0:T(1024)S(1)} %get-tuple-element.25), kind=kOutput, calls=%fused_computation.16 | convolution fusion | flops 2153775104 | bytes 6299648 | tf_op jit(solution)/shard_map/dot_general | solution.py:35
  119.5 3.9 %copy.19 = bf16[1024,1024]{0,1:T(8,128)(2,1)} copy(bf16[1024,1024]{1,0:T(8,128)(2,1)} %multiply_convert_fusion) | data formatting | bytes 4194304
  123.4 0.0 reduce-scatter.7.cloned.1.call-update
  123.4 0.2 all-gather.5.cloned.1.call-start
  123.7 61.3 %reduce-scatter.5.cloned.1.call-done = bf16[32,1024]{1,0:T(8,128)(2,1)} async-done(((bf16[1024,1024]{1,0:T(8,128)(2,1)}), bf16[32,1024]{1,0:T(8,128)(2,1)}) %reduce-scatter.5.cloned.1.call-update) | async-done | bytes 65552 | tf_op jit(solution)/shard_map/reduce_scatter | solution.py:55
  185.0 0.0 copy-done
  185.0 0.0 copy-done.1
  185.0 1.6 fusion.17
  186.6 0.0 all-gather.5.cloned.1.call-update
  186.6 4.6 %fusion.6 = bf16[1024,1024]{0,1:T(8,128)(2,1)} fusion(bf16[1024,1024]{0,1:T(8,128)(2,1)S(1)} %copy.16, f32[1024,1024]{0,1:T(8,128)} %get-tuple-element.26, f32[1024]{0:T(1024)S(1)} %get-tuple-element.18, f32[1024]{0:T(1024)S(1)} %get-tuple-element.24, f32[1024]{0:T(1024)S(1)} %broadcast_multiply_fusion, f32[1024]{0:T(1024)S(1)} %get-tuple-element.25), kind=kLoop, calls=%fused_computation.10 | loop fusion | flops 8388608 | bytes 8404992 | tf_op jit(solution)/shard_map/convert_element_type | solution.py:52
  191.2 3.9 %copy.18 = bf16[1024,1024]{1,0:T(8,128)(2,1)} copy(bf16[1024,1024]{0,1:T(8,128)(2,1)} %fusion.6) | data formatting | bytes 4194304
  195.1 94.8 %reduce-scatter.7.cloned.1.call-done = bf16[128,1024]{1,0:T(8,128)(2,1)} async-done(((bf16[1024,1024]{1,0:T(8,128)(2,1)}), bf16[128,1024]{1,0:T(8,128)(2,1)}) %reduce-scatter.7.cloned.1.call-update) | async-done | bytes 262160
  289.9 1.8 copy.20
  291.7 58.5 %all-gather.5.cloned.1.call-done = bf16[1024,1024]{1,0:T(8,128)(2,1)} async-done(((bf16[32,1024]{1,0:T(8,128)(2,1)}), bf16[1024,1024]{1,0:T(8,128)(2,1)}) %all-gather.5.cloned.1.call-update) | async-done | bytes 2097168 | tf_op jit(solution)/shard_map/all_gather | solution.py:65
  350.2 6.7 %fusion.13 = bf16[1,1024,1024]{2,1,0:T(8,128)(2,1)} fusion(bf16[1024,1024]{1,0:T(8,128)(2,1)} %all-gather.3.cloned.1.call-done, bf16[1024,1024]{1,0:T(8,128)(2,1)} %all-gather.5.cloned.1.call-done, bf16[1,1024,1024]{2,1,0:T(8,128)(2,1)} %param.11, bf16[1024,1024]{0,1:T(8,128)(2,1)S(1)} %copy.16, f32[1024]{0:T(1024)S(1)} %copy-done.2, ...), kind=kOutput, calls=%fused_computation.23 | convolution fusion | flops 2159017984 | bytes 10493952 | tf_op jit(solution)/shard_map/dot_general | solution.py:42
  (4 shorter events, 0.0 us)
Async XLA Ops:
  8.0 76.6 %all-gather.3.cloned.1.call-start = ((), (), s32[]{:S(2)}) async-start(), calls=%async_computation.2 | async-start | bytes 2359296 | tf_op jit(solution)/shard_map/all_gather | solution.py:40
  8.7 176.3 %reduce-scatter.5.cloned.1.call-start = ((), (), s32[]{:S(2)}) async-start(), calls=%async_computation.3 | async-start | bytes 2162688 | tf_op jit(solution)/shard_map/reduce_scatter | solution.py:55
  24.1 2.9 copy-start.2
  24.1 265.8 %reduce-scatter.7.cloned.1.call-start = ((), (), s32[]{:S(2)}) async-start(), calls=%async_computation.5 | async-start | bytes 2359296
  123.4 61.6 %copy-start = (f32[1,32,1024]{2,1,0:T(8,128)S(1)}, f32[1,32,1024]{2,1,0:T(8,128)}, u32[]{:S(2)}) copy-start(f32[1,32,1024]{2,1,0:T(8,128)} %param.15) | copy-start | bytes 393220
  123.4 61.6 %copy-start.1 = (f32[1,32,1024]{2,1,0:T(8,128)S(1)}, f32[1,32,1024]{2,1,0:T(8,128)}, u32[]{:S(2)}) copy-start(f32[1,32,1024]{2,1,0:T(8,128)} %param.14) | copy-start | bytes 393220
  123.4 226.8 %all-gather.5.cloned.1.call-start = ((), (), s32[]{:S(2)}) async-start(), calls=%async_computation.4 | async-start | bytes 2162688 | tf_op jit(solution)/shard_map/all_gather | solution.py:65
Sparse Core Ops, SparseCore 0:
  11.6 72.9 all-gather.2
Sparse Core Ops, SparseCore 1:
  24.2 160.8 reduce-scatter.4
  189.5 100.4 reduce-scatter.6
  291.7 58.5 all-gather.4
where the time goes:
time: 365 us
  waiting for transfers between devices  273 us (75%)
  blocking collectives  22.8 us (6%)
  local copies, waits for them, and re-layouts  20 us (5%)
  matrix products  18.8 us (5%)
  between operations  15.7 us (4%)
  other arithmetic  13.9 us (4%)
    unnamed x5, waiting for transfers between devices  95.6 us
    reduce_scatter x1, waiting for transfers between devices, local(): lax.psum_scatter(decode(words, scales).astype(jnp.bfloat16), 'rep', scatt...  61.3 us
    all_gather x1, waiting for transfers between devices, local(): lax.all_gather(shared, 'rep', axis=0, tiled=True).astype(jnp.float32)  58.5 us
    all_gather x1, waiting for transfers between devices, local(): piece = lax.all_gather(cotangent, 'tp', axis=1, tiled=True)  57.5 us
    psum x1, blocking collectives, local(): squares = lax.psum(jnp.sum(wide * wide, axis=-1), 'tp')  22.8 us
    unnamed x11, local copies, waits for them, and re-layouts  14.5 us
  transfers between devices with their start and end apart: 4, of which 4 were waited for; matrix products, arithmetic and copies ran while one was open for 13% of the time, Pallas kernels for 0%

commit v1 on v0

v1 whole, which is shorter than its diff:
```python
import math

import jax
import jax.numpy as jnp
from jax import lax
from jax.experimental import pallas as pl
from jax.experimental.pallas import tpu as pltpu
from jax.sharding import PartitionSpec as P

MESH = pl.DeviceIdType.MESH
BF = jnp.bfloat16
F32 = jnp.float32

D = 8192
T = 1024
F = 1024
C = 1024
H = 512
L = 128
FACTOR = 1.0 / math.sqrt(D)

epsilon = 1e-05
outer_rate = 0.7
outer_push = 0.9
keep_share = 0.5
inner_rate = 0.5

SEMS = 96


def row_of(ref):
    return jnp.concatenate([ref[pl.ds(i, 1), :] for i in range(8)], axis=1)


def store_row(ref, row):
    for i in range(8):
        ref[pl.ds(i, 1), :] = row[:, i * L:(i + 1) * L]


def to_row(column_sums):
    return jnp.sum(jnp.transpose(column_sums), axis=0, keepdims=True)


def to_column(row):
    return jnp.transpose(jnp.broadcast_to(row, (L, T)))


def kernel(
    x_hbm, gain_hbm, cot_hbm, w_hbm, codes_hbm, scales_hbm, glob_hbm, mom_hbm,
    proj_hbm, gx_hbm, nl_hbm, ng_hbm, nm_hbm,
    x_v, gain_v, w_v, codes_v, scales_v, glob_v, mom_v,
    xg, xgt, cotf, csf, pf, pn, pown, ar, br, cr, zsend, zrecv,
    cores, corer, xs, xr, zs, zr, zown, sh,
    acc, invb, coefb, sqs, sqr, sqz, sqzr, ins, inr, inz, inzr,
    gn, gw, gx, nl, proj, ng, nm,
    send_sem, recv_sem, load_sem, out_sem,
):
    rep = lax.axis_index("rep")
    tp = lax.axis_index("tp")
    zl = rep // 8
    xx = (rep // 2) % 4
    c = rep % 2
    zh = tp // 4
    y = tp % 4

    def at_y(d):
        return (rep, zh * 4 + (y + d) % 4)

    def at_x(d):
        return (zl * 8 + ((xx + d) % 4) * 2 + c, tp)

    def at_z(d):
        return (((zl + d) % 4) * 8 + xx * 2 + c, tp)

    at_zh = (rep, (1 - zh) * 4 + y)
    at_core = (zl * 8 + xx * 2 + (1 - c), tp)

    counter = [0]

    def remote(src, dst, dev, landing=None):
        i = counter[0]
        counter[0] += 1
        send = pltpu.make_async_remote_copy(
            src_ref=src, dst_ref=dst, send_sem=send_sem.at[i], recv_sem=recv_sem.at[i],
            device_id=dev, device_id_type=MESH,
        )
        if landing is None:
            return send, send
        recv = pltpu.make_async_remote_copy(
            src_ref=src, dst_ref=landing, send_sem=send_sem.at[i], recv_sem=recv_sem.at[i],
            device_id=dev, device_id_type=MESH,
        )
        return send, recv

    sent = []

    def go(pair):
        pair[0].start()
        sent.append(pair[0])

    loads = {}
    for i, (name, src, dst) in enumerate((
        ("codes", codes_hbm, codes_v), ("scales", scales_hbm, scales_v),
        ("cot", cot_hbm, cotf.at[tp]), ("x", x_hbm, x_v), ("gain", gain_hbm, gain_v),
        ("w", w_hbm, w_v), ("glob", glob_hbm, glob_v), ("mom", mom_hbm, mom_v),
    )):
        loads[name] = pltpu.make_async_copy(src, dst, load_sem.at[i])
        loads[name].start()

    barrier = pltpu.get_barrier_semaphore()
    peers = [at_y(1), at_y(2), at_y(3), at_zh, at_core]
    peers += [at_x(d) for d in (1, 2, 3)] + [at_z(d) for d in (1, 2, 3)]
    for dev in peers:
        pl.semaphore_signal(barrier, inc=1, device_id=dev, device_id_type=MESH)

    def decoded(block, k):
        rows = pl.ds(pl.multiple_of(block * 32, 32), 32)
        words = codes_v[rows, :]
        codes = (jnp.bitwise_and(jnp.right_shift(words, 4 * k), 15) - 8).astype(F32)
        scales = scales_v[rows, :]
        return jnp.concatenate(
            [codes[:, g * L:(g + 1) * L] * scales[:, 4 * k + g:4 * k + g + 1] for g in range(4)], axis=1
        )

    loads["codes"].wait()
    loads["scales"].wait()
    offsets = (2, 1, 3, 0)

    for k in range(2):
        def for_partner(i, carry, k=k):
            cores[k, i // 4, i % 4] = decoded((i % 4) * 8 + (i // 4) * 2 + (1 - c), k).astype(BF)
            return carry
        lax.fori_loop(0, 16, for_partner, 0)

    loads["cot"].wait()
    pl.semaphore_wait(barrier, len(peers))

    other = (1 - zh) * 4 + y

    def block_of(half, d):
        return half * 4 + (y + d) % 4

    cot_z = remote(cotf.at[tp], cotf.at[tp], at_zh, cotf.at[other])
    cot_near = [
        remote(cotf.at[tp], cotf.at[tp], at_y(1), cotf.at[block_of(zh, 3)]),
        remote(cotf.at[tp], cotf.at[tp], at_y(3), cotf.at[block_of(zh, 1)]),
    ]
    go(cot_z)
    go(cot_near[0])
    go(cot_near[1])

    core_copies = {}
    for k in range(2):
        for d in offsets:
            xi = (xx + d) % 4
            core_copies[k, d] = remote(cores.at[k, xi], corer.at[k, xi], at_core)
            go(core_copies[k, d])

    loads["gain"].wait()
    loads["x"].wait()
    gain = gain_v[...]

    def scale_rows(i, carry):
        rows = pl.ds(pl.multiple_of(i * 32, 32), 32)
        wide = x_v[rows, :].astype(F32)
        xg[rows, :] = (wide * gain).astype(BF)
        squares = wide * wide
        total = squares[:, 0:L]
        for j in range(1, 8):
            total = total + squares[:, j * L:(j + 1) * L]
        acc[rows, :] = total
        return carry
    lax.fori_loop(0, 32, scale_rows, 0)
    loads["w"].wait()

    halves = (pl.ds(0, H), pl.ds(H, H))

    def weights(target):
        first = pl.ds(pl.multiple_of(((1 - zh) * 4 + target) * L, L), L)
        second = pl.ds(pl.multiple_of((zh * 4 + target) * L, L), L)
        return jnp.concatenate([w_v[:, first], w_v[:, second]], axis=1)

    def project(rows, cols):
        return jnp.dot(xg[rows, :], cols, preferred_element_type=F32)

    cols = weights((y + 2) % 4)
    far = {}
    for d in range(2):
        value = project(halves[d], cols)
        for q in range(2):
            pf[q, halves[d], :] = value[:, q * L:(q + 1) * L].astype(BF)
        for q in range(2):
            far[d, q] = remote(pf.at[q, halves[d]], ar.at[d, q], at_y((1, 3)[d]))
            go(far[d, q])

    store_row(sqs, to_row(acc[...]))
    sq_y = [remote(sqs, sqr.at[d - 1], at_y(d)) for d in (1, 2, 3)]
    for pair in sq_y:
        go(pair)

    x_copies = {}
    for k in range(2):
        for d in offsets:
            xi = (xx + d) % 4
            core_copies[k, d][1].wait_recv()

            def add_partner(zi, carry, k=k, xi=xi):
                both = decoded(zi * 8 + xi * 2 + c, k) + corer[k, xi, zi].astype(F32)
                xs[k, xi, zi] = both.astype(BF)
                return carry
            lax.fori_loop(0, 4, add_partner, 0)
            if d:
                x_copies[k, d] = remote(xs.at[k, xi], xr.at[k, d - 1], at_x(d))
                go(x_copies[k, d])

    near = {}
    for d in range(2):
        cols = weights((y + (1, 3)[d]) % 4)
        for h in (1 - d, d):
            value = project(halves[h], cols)
            for q in range(2):
                pn[d, q, halves[h], :] = value[:, q * L:(q + 1) * L].astype(BF)
            if h == 1 - d:
                for q in range(2):
                    near[d, q] = remote(pn.at[d, q, halves[h]], cr.at[d, q], at_y((1, 3)[d]))
                    go(near[d, q])

    onward = {}
    for q in range(2):
        for d in range(2):
            far[d, q][1].wait_recv()
            pn[d, q, halves[d], :] = (
                pn[d, q, halves[d], :].astype(F32) + ar[d, q].astype(F32)
            ).astype(BF)
            onward[d, q] = remote(pn.at[d, q, halves[d]], br.at[d, q], at_y((1, 3)[d]))
            go(onward[d, q])

    cols = weights(y)
    for h in range(2):
        value = project(halves[h], cols)
        for q in range(2):
            pown[q, halves[h], :] = value[:, q * L:(q + 1) * L]

    for pair in sq_y:
        pair[1].wait_recv()
    sqz[...] = sqs[...] + sqr[0] + sqr[1] + sqr[2]
    sq_z = remote(sqz, sqzr, at_zh)
    go(sq_z)

    def along_x(k):
        for d in (1, 2, 3):
            x_copies[k, d][1].wait_recv()

        def add(zi, carry, k=k):
            total = xs[k, xx, zi].astype(F32)
            for s in range(3):
                total = total + xr[k, s, zi].astype(F32)
            zs[k, zi] = total.astype(BF)
            return carry
        lax.fori_loop(0, 4, add, 0)
        copies = []
        for d in (2, 1, 3):
            copies.append(remote(zs.at[k, (zl + d) % 4], zr.at[k, d - 1], at_z(d)))
            go(copies[-1])
        return copies

    def outer(k, copies):
        for pair in copies:
            pair[1].wait_recv()
        total = zs[k, zl].astype(F32)
        for s in range(3):
            total = total + zr[k, s].astype(F32)
        delta = total * (1.0 / 32.0)
        part = pl.ds(k * H, H)
        new_momentum = outer_push * mom_v[:, part] + delta
        new_global = glob_v[:, part] - outer_rate * (delta + outer_push * new_momentum)
        nm[:, part] = new_momentum
        ng[:, part] = new_global
        sh[k, c, xx, zl] = new_global.astype(BF)
        copies = []
        for d in (2, 1, 3):
            here = sh.at[k, c, xx, zl]
            copies.append(remote(here, here, at_z(d), sh.at[k, c, xx, (zl - d + 4) % 4]))
            go(copies[-1])
        return copies

    def spread_x(k, copies):
        for pair in copies:
            pair[1].wait_recv()
        here = sh.at[k, c, xx]
        copies = {}
        for d in (2, 1, 3):
            copies[d] = remote(here, here, at_x(d), sh.at[k, c, (xx - d + 4) % 4])
            go(copies[d])
        copies[0] = remote(here, here, at_core, sh.at[k, 1 - c, xx])
        go(copies[0])
        return copies

    def spread_core(k, copies):
        arrivals = [copies[0]]
        for d in (1, 3, 2):
            copies[d][1].wait_recv()
            xi = (xx - d + 4) % 4
            here = sh.at[k, c, xi]
            arrivals.append(remote(here, here, at_core, sh.at[k, 1 - c, xi]))
            go(arrivals[-1])
        return arrivals

    z0 = along_x(0)

    cot_far = []
    for d in range(2):
        cot_near[d][1].wait_recv()
        came = block_of(zh, (3, 1)[d])
        part = cotf.at[came, halves[d]]
        cot_far.append(remote(part, part, at_y((1, 3)[d]), cotf.at[block_of(zh, 2), halves[d]]))
        go(cot_far[-1])
    cot_z[1].wait_recv()
    other_near = []
    for d in range(2):
        here = cotf.at[other]
        other_near.append(remote(here, here, at_y((1, 3)[d]), cotf.at[block_of(1 - zh, (3, 1)[d])]))
        go(other_near[-1])

    for j in range(4):
        xgt[pl.ds(j * 256, 256), :] = jnp.transpose(xg[:, pl.ds(j * 256, 256)])

    loads["glob"].wait()
    loads["mom"].wait()
    z1 = along_x(1)
    z0 = outer(0, z0)

    for h in range(2):
        onward[h, 0][1].wait_recv()
        near[1 - h, 0][1].wait_recv()
        total = pown[0, halves[h], :] + br[h, 0].astype(F32) + cr[1 - h, 0].astype(F32)
        zsend[halves[h], :] = total.astype(BF)
        acc[halves[h], :] = total * cotf[other, halves[h], :].astype(F32)
    proj_z = remote(zsend, zrecv, at_zh)
    go(proj_z)

    z1 = outer(1, z1)
    x0 = spread_x(0, z0)

    for h in range(2):
        onward[h, 1][1].wait_recv()
        near[1 - h, 1][1].wait_recv()
        total = pown[1, halves[h], :] + br[h, 1].astype(F32) + cr[1 - h, 1].astype(F32)
        pown[1, halves[h], :] = total
        acc[halves[h], :] = acc[halves[h], :] + total * cotf[tp, halves[h], :].astype(F32)
    store_row(ins, to_row(acc[...]))
    in_y = [remote(ins, inr.at[d - 1], at_y(d)) for d in (1, 2, 3)]
    for pair in in_y:
        go(pair)

    x1 = spread_x(1, z1)

    sq_z[1].wait_recv()
    squares = row_of(sqz) + row_of(sqzr)
    inverse = lax.rsqrt(squares * (1.0 / D) + epsilon)
    invb[...] = to_column(inverse)

    for pair in cot_far:
        pair[1].wait_recv()

    def group(half, first):
        for j in range(4):
            csf[half * 4 + j] = (cotf[half * 4 + j].astype(F32) * invb[...]).astype(BF)

        def weight_part(j, carry):
            right = jnp.concatenate([csf[half * 4 + 2 * j], csf[half * 4 + 2 * j + 1]], axis=1)
            part = pl.ds(pl.multiple_of(j * 256, 256), 256)
            gw[half, :, part] = jnp.dot(xgt[...], right, preferred_element_type=F32)
            return carry
        lax.fori_loop(0, 2, weight_part, 0)

    def normed_part(half, j):
        left = jnp.concatenate([cotf[half * 4 + i] for i in range(4)], axis=1)
        rows = pl.ds(pl.multiple_of(j * 256, 256), 256)
        right = w_v[rows, pl.ds(pl.multiple_of(half * H, H), H)]
        return lax.dot_general(left, right, (((1,), (1,)), ((), ())), preferred_element_type=F32)

    def keep_part(j, carry):
        gn[j] = normed_part(zh, j)
        return carry
    lax.fori_loop(0, 4, keep_part, 0)
    group(zh, True)

    for pair in in_y:
        pair[1].wait_recv()
    inz[...] = ins[...] + inr[0] + inr[1] + inr[2]
    in_z = remote(inz, inzr, at_zh)
    go(in_z)

    other_far = []
    for d in range(2):
        other_near[d][1].wait_recv()
        came = block_of(1 - zh, (3, 1)[d])
        part = cotf.at[came, halves[d]]
        other_far.append(remote(part, part, at_y((1, 3)[d]), cotf.at[block_of(1 - zh, 2), halves[d]]))
        go(other_far[-1])

    c0 = spread_core(0, x0)

    proj_z[1].wait_recv()
    proj[...] = ((pown[1] + zrecv[...].astype(F32)) * invb[...] * FACTOR).astype(BF)
    outs = [
        pltpu.make_async_copy(proj, proj_hbm, out_sem.at[0]),
        pltpu.make_async_copy(ng, ng_hbm, out_sem.at[1]),
        pltpu.make_async_copy(nm, nm_hbm, out_sem.at[2]),
    ]
    for copy in outs:
        copy.start()

    c1 = spread_core(1, x1)

    in_z[1].wait_recv()
    inner = row_of(inz) + row_of(inzr)
    coefb[...] = to_column(inverse * inverse * inverse * inner * (FACTOR / D))
    for pair in other_far:
        pair[1].wait_recv()

    def finish_x(j, carry):
        part = pl.ds(pl.multiple_of(j * 256, 256), 256)
        value = (gn[j] + normed_part(1 - zh, j)) * (gain_v[:, part] * FACTOR)
        scale = jnp.concatenate([invb[...]] * 2, axis=1)
        coef = jnp.concatenate([coefb[...]] * 2, axis=1)
        gx[:, part] = (value * scale - x_v[:, part].astype(F32) * coef).astype(BF)
        copy = pltpu.make_async_copy(gx.at[:, part], gx_hbm.at[:, part], out_sem.at[4 + j])
        copy.start()
        return carry
    lax.fori_loop(0, 4, finish_x, 0)

    group(1 - zh, False)
    for k, arrivals in ((0, c0), (1, c1)):
        for pair in arrivals:
            pair[1].wait_recv()

    def finish_w(b, carry):
        rows = pl.ds(pl.multiple_of(b * 32, 32), 32)
        for k in range(2):
            part = pl.ds(k * H, H)
            mixed = (
                keep_share * w_v[rows, part].astype(F32)
                + (1.0 - keep_share) * sh[k, b % 2, (b // 2) % 4, b // 8].astype(F32)
                - (inner_rate * FACTOR) * gw[k, rows, :]
            )
            nl[rows, part] = mixed.astype(BF)
        return carry

    for q in range(4):
        lax.fori_loop(8 * q, 8 * q + 8, finish_w, 0)
        rows = pl.ds(q * 256, 256)
        copy = pltpu.make_async_copy(nl.at[rows], nl_hbm.at[rows], out_sem.at[8 + q])
        copy.start()
        outs.append(copy)
    for j in range(4):
        part = pl.ds(j * 256, 256)
        outs.append(pltpu.make_async_copy(gx.at[:, part], gx_hbm.at[:, part], out_sem.at[4 + j]))
    for copy in outs:
        copy.wait()
    for copy in sent:
        copy.wait_send()
    assert counter[0] <= SEMS


def local(
    tokens_in, gain, cotangent, local_weight, packed_codes, code_scales, global_weight, momentum
):
    any_ = pl.BlockSpec(memory_space=pl.ANY)
    vm = pltpu.VMEM
    projected, grad_x, new_local, new_global, new_momentum = pl.pallas_call(
        kernel,
        out_shape=(
            jax.ShapeDtypeStruct((T, L), BF),
            jax.ShapeDtypeStruct((T, F), BF),
            jax.ShapeDtypeStruct((F, C), BF),
            jax.ShapeDtypeStruct((32, C), F32),
            jax.ShapeDtypeStruct((32, C), F32),
        ),
        in_specs=[any_] * 8,
        out_specs=[any_] * 5,
        scratch_shapes=[
            vm((T, F), BF), vm((1, F), F32), vm((F, C), BF), vm((F, C // 2), jnp.int32), vm((F, 8), F32),
            vm((32, C), F32), vm((32, C), F32),
            vm((T, F), BF), vm((F, T), BF), vm((8, T, L), BF), vm((8, T, L), BF),
            vm((2, T, L), BF), vm((2, 2, T, L), BF), vm((2, T, L), F32),
            vm((2, 2, H, L), BF), vm((2, 2, H, L), BF), vm((2, 2, H, L), BF),
            vm((T, L), BF), vm((T, L), BF),
            vm((2, 4, 4, 32, H), BF), vm((2, 4, 4, 32, H), BF), vm((2, 4, 4, 32, H), BF),
            vm((2, 3, 4, 32, H), BF), vm((2, 4, 32, H), BF), vm((2, 3, 32, H), BF), vm((8, L), F32),
            vm((2, 2, 4, 4, 32, H), BF),
            vm((T, L), F32), vm((T, L), F32), vm((T, L), F32),
            vm((8, L), F32), vm((3, 8, L), F32), vm((8, L), F32), vm((8, L), F32),
            vm((8, L), F32), vm((3, 8, L), F32), vm((8, L), F32), vm((8, L), F32),
            vm((4, T, 256), F32), vm((2, F, H), F32), vm((T, F), BF), vm((F, C), BF),
            vm((T, L), BF), vm((32, C), F32), vm((32, C), F32),
            pltpu.SemaphoreType.DMA((SEMS,)), pltpu.SemaphoreType.DMA((SEMS,)),
            pltpu.SemaphoreType.DMA((8,)), pltpu.SemaphoreType.DMA((12,)),
        ],
        compiler_params=pltpu.CompilerParams(
            collective_id=0, has_side_effects=True, vmem_limit_bytes=60 * 2**20
        ),
        cost_estimate=pl.CostEstimate(flops=6 * 2**30, bytes_accessed=12 * 2**20, transcendentals=0),
    )(
        tokens_in, gain.reshape(1, F), cotangent, local_weight[0], packed_codes[0], code_scales[0],
        global_weight[0], momentum[0],
    )
    return (projected, grad_x, new_local[None], new_global[None], new_momentum[None])


def solution(mesh):
    return jax.shard_map(
        local,
        mesh=mesh,
        in_specs=(
            P("rep", "tp"),
            P("tp"),
            P("rep", "tp"),
            P("rep", "tp", None),
            P("rep", "tp", None),
            P("rep", "tp", None),
            P("tp", "rep", None),
            P("tp", "rep", None),
        ),
        out_specs=(
            P("rep", "tp"),
            P("rep", "tp"),
            P("rep", "tp", None),
            P("tp", "rep", None),
            P("tp", "rep", None),
        ),
        check_vma=False,
    )
```

time: 365 us -> 75.8 us (0.21)
  waiting for transfers between devices: 273 us -> 0 us
  Pallas kernels: 0 us -> 65 us
  blocking collectives: 22.8 us -> 0 us
  matrix products: 18.8 us -> 0 us
  between operations: 15.7 us -> 0.64 us
  other arithmetic: 13.9 us -> 0 us
  local copies, waits for them, and re-layouts: 20 us -> 9.3 us
    all_gather x2 -> x0, waiting for transfers between devices: 116 us -> none  [the longest x1 58.5 us: local(): lax.all_gather(shared, 'rep', axis=0, tiled=True).astype(jnp.float32)]
    unnamed x5 -> x0, waiting for transfers between devices: 95.6 us -> none
    pallas_call x0 -> x1, Pallas kernels: none -> 65 us  [local(): pl.pallas_call(kernel, out_shape=(jax.ShapeDtypeStruct((T, L), BF), jax.S...]
    reduce_scatter x1 -> x0, waiting for transfers between devices: 61.3 us -> none  [local(): lax.psum_scatter(decode(words, scales).astype(jnp.bfloat16), 'rep', scatt...]
    psum x1 -> x0, blocking collectives: 22.8 us -> none  [local(): squares = lax.psum(jnp.sum(wide * wide, axis=-1), 'tp')]
    dot_general x3 -> x0, matrix products: 18.8 us -> none  [the longest x1 6.73 us: local(): lax.dot_general(normed, piece, (((0,), (0,)), ((), ())), preferred_elemen...]
    convert_element_type x2 -> x0, other arithmetic: 8.8 us -> none  [the longest x1 4.56 us: local(): (inverse * scaled - wide * inverse ** 3 * inner / D).astype(jnp.bfloat16)]
    unnamed x11 -> x12, local copies, waits for them, and re-layouts: 14.5 us -> 9.3 us
  transfers between devices with their start and end apart: 4 -> 0, of which waited for: 4 -> 0; matrix products, arithmetic and copies ran while one was open for 13% -> 0% of each run, Pallas kernels for 0% -> 0%
where the time goes in v1:
time: 75.8 us; the launch traced here: 75 us
  Pallas kernels  65 us (86%)
  local copies, waits for them, and re-layouts  9.3 us (12%)
    pallas_call x1, Pallas kernels, local(): pl.pallas_call(kernel, out_shape=(jax.ShapeDtypeStruct((T, L), BF), jax.S...  65 us
    unnamed x12, local copies, waits for them, and re-layouts  9.3 us

profile of v1, /device:TPU:1, one launch (start us, length us, event | category | flops | bytes accessed | tf_op | source)
XLA Modules:
  0.0 75.0 jit_solution(3800236622968191769)
XLA Ops:
  0.6 1.8 %copy.13 = f32[1,1024,8]{2,1,0:T(8,128)} copy(f32[1,1024,8]{1,2,0:T(8,128)} %param.13) | data formatting | bytes 65536 | tf_op args[5]
  2.4 65.0 %shard_map.119 = (bf16[1024,128]{1,0:T(8,128)(2,1)}, bf16[1024,1024]{1,0:T(8,128)(2,1)}, bf16[1024,1024]{1,0:T(8,128)(2,1)}, f32[32,1024]{1,0:T(8,128)}, f32[32,1024]{1,0:T(8,128)}) custom-call(bf16[1024,1024]{1,0:T(8,128)(2,1)} %x_hbm.1, f32[1,1024]{1,0:T(1,128)} %bitcast.17, bf16[1024,128]{1,0:T(8,128)(2,1)} %cot_hbm.1, bf16[1024,1024]{1,0:T(8,128)(2,1)} %bitcast.13, ...), custom_call_target="tpu_custom_call" | custom-call | flops 6442450944 | bytes 12582912 | tf_op jit(solution)/shard_map/pallas_call | solution.py:472
  67.4 1.7 %copy.19 = bf16[1024,128]{1,0:T(8,128)(2,1)} copy(bf16[1024,128]{1,0:T(8,128)(2,1)} %get-tuple-element.20) | data formatting | bytes 524288
  69.1 0.0 copy-start
  69.1 3.2 %copy.20 = bf16[1024,1024]{1,0:T(8,128)(2,1)} copy(bf16[1024,1024]{1,0:T(8,128)(2,1)} %get-tuple-element.21) | data formatting | bytes 4194304
  72.3 0.0 copy-done
  72.3 0.0 copy-start.2
  72.3 0.0 copy-start.1
  72.3 1.3 %copy.21 = bf16[1,1024,1024]{2,1,0:T(8,128)(2,1)} copy(bf16[1,1024,1024]{2,1,0:T(8,128)(2,1)S(1)} %bitcast.9) | data formatting | bytes 4194304
  73.7 0.0 copy-done.2
  73.7 0.7 copy.22
  74.3 0.0 copy-done.1
  74.3 0.7 copy.23
Async XLA Ops:
  69.1 3.2 %copy-start = (bf16[1024,1024]{1,0:T(8,128)(2,1)S(1)}, bf16[1024,1024]{1,0:T(8,128)(2,1)}, u32[]{:S(2)}) copy-start(bf16[1024,1024]{1,0:T(8,128)(2,1)} %get-tuple-element.12) | copy-start | bytes 6291460
  72.3 1.3 %copy-start.2 = (f32[32,1024]{1,0:T(8,128)S(1)}, f32[32,1024]{1,0:T(8,128)}, u32[]{:S(2)}) copy-start(f32[32,1024]{1,0:T(8,128)} %get-tuple-element.13) | copy-start | bytes 393220
  72.3 2.0 %copy-start.1 = (f32[32,1024]{1,0:T(8,128)S(1)}, f32[32,1024]{1,0:T(8,128)}, u32[]{:S(2)}) copy-start(f32[32,1024]{1,0:T(8,128)} %get-tuple-element.14) | copy-start | bytes 393220

commit v2 on v0

v2 whole, which is shorter than its diff:
```python
import math

import jax
import jax.numpy as jnp
from jax import lax
from jax.experimental import pallas as pl
from jax.experimental.pallas import tpu as pltpu
from jax.sharding import PartitionSpec as P

MESH = pl.DeviceIdType.MESH
BF = jnp.bfloat16
F32 = jnp.float32

D = 8192
T = 1024
F = 1024
C = 1024
H = 512
L = 128
FACTOR = 1.0 / math.sqrt(D)

epsilon = 1e-05
outer_rate = 0.7
outer_push = 0.9
keep_share = 0.5
inner_rate = 0.5

SEMS = 48


def row_of(ref):
    return jnp.concatenate([ref[pl.ds(i, 1), :] for i in range(8)], axis=1)


def store_row(ref, row):
    for i in range(8):
        ref[pl.ds(i, 1), :] = row[:, i * L:(i + 1) * L]


def to_row(column_sums):
    return jnp.sum(jnp.transpose(column_sums), axis=0, keepdims=True)


def to_column(row):
    return jnp.transpose(jnp.broadcast_to(row, (L, T)))


def kernel(
    x_hbm, gain_hbm, cot_hbm, w_hbm, codes_hbm, scales_hbm, glob_hbm, mom_hbm,
    proj, gx, nl, ng, nm,
    x_v, gain_v, w_v, codes_v, scalest_v, scales_v, glob_v, mom_v,
    xg, xgt, cotf, csf, pf, pn, pown, ar, br, cr, zsend, zrecv,
    cores, corer, xs, xr, zs, zr, zown, sh,
    acc, invb, coefb, sqs, sqr, sqz, sqzr, ins, inr, inz, inzr,
    gn, gw,
    send_sem, recv_sem, load_sem,
):
    rep = lax.axis_index("rep")
    tp = lax.axis_index("tp")
    zl = rep // 8
    xx = (rep // 2) % 4
    c = rep % 2
    zh = tp // 4
    y = tp % 4

    def at_y(d):
        return (rep, zh * 4 + (y + d) % 4)

    def at_x(d):
        return (zl * 8 + ((xx + d) % 4) * 2 + c, tp)

    def at_z(d):
        return (((zl + d) % 4) * 8 + xx * 2 + c, tp)

    at_zh = (rep, (1 - zh) * 4 + y)
    at_core = (zl * 8 + xx * 2 + (1 - c), tp)

    slots = {"send": {}, "recv": {}}

    def slot(kind, key):
        return slots[kind].setdefault(key, len(slots[kind]))

    def describe(src, dst, dev, send_key, recv_key):
        return pltpu.make_async_remote_copy(
            src_ref=src, dst_ref=dst,
            send_sem=send_sem.at[slot("send", send_key)], recv_sem=recv_sem.at[slot("recv", recv_key)],
            device_id=dev, device_id_type=MESH,
        )

    def go(src, dst, dev, send_key, recv_key):
        describe(src, dst, dev, send_key, recv_key).start()

    def arrived(recv_key, like):
        describe(like, like, at_core, "none", recv_key).wait_recv()

    def departed(send_key, like):
        describe(like, like, at_core, send_key, "none").wait_send()

    loads = {}
    for i, (name, src, dst) in enumerate((
        ("scales", scales_hbm, scalest_v), ("codes", codes_hbm, codes_v),
        ("cot", cot_hbm, cotf.at[tp]), ("gain", gain_hbm, gain_v), ("x", x_hbm, x_v),
        ("w", w_hbm, w_v), ("glob", glob_hbm, glob_v), ("mom", mom_hbm, mom_v),
    )):
        loads[name] = pltpu.make_async_copy(src, dst, load_sem.at[i])
        loads[name].start()

    barrier = pltpu.get_barrier_semaphore()
    peers = [at_y(1), at_y(2), at_y(3), at_zh, at_core]
    peers += [at_x(d) for d in (1, 2, 3)] + [at_z(d) for d in (1, 2, 3)]
    for dev in peers:
        pl.semaphore_signal(barrier, inc=1, device_id=dev, device_id_type=MESH)

    def half_of(k):
        return zh if k == 0 else 1 - zh

    def columns_of(k):
        return pl.ds(pl.multiple_of(half_of(k) * H, H), H)

    def decoded(block, k):
        rows = pl.ds(pl.multiple_of(block * 32, 32), 32)
        words = codes_v[rows, :]
        codes = (jnp.bitwise_and(jnp.right_shift(words, 4 * half_of(k)), 15) - 8).astype(F32)
        scales = scales_v[k, rows, :]
        return jnp.concatenate(
            [codes[:, g * L:(g + 1) * L] * scales[:, g:g + 1] for g in range(4)], axis=1
        )

    offsets = (2, 1, 3, 0)
    near_dev = (at_y(1), at_y(3))
    halves = (pl.ds(0, H), pl.ds(H, H))
    other = (1 - zh) * 4 + y

    def block_of(half, d):
        return half * 4 + (y + d) % 4

    loads["scales"].wait()
    all_scales = jnp.transpose(scalest_v[...])
    first, second = all_scales[:, 0:4], all_scales[:, 4:8]
    scales_v[0] = jnp.where(zh == 0, first, second)
    scales_v[1] = jnp.where(zh == 0, second, first)
    loads["codes"].wait()
    for k in range(2):
        def for_partner(i, carry, k=k):
            cores[k, i // 4, i % 4] = decoded((i % 4) * 8 + (i // 4) * 2 + (1 - c), k).astype(BF)
            return carry
        lax.fori_loop(0, 16, for_partner, 0, unroll=4)

    loads["gain"].wait()
    loads["x"].wait()
    gain = gain_v[...]

    def scale_rows(i, carry):
        rows = pl.ds(pl.multiple_of(i * 32, 32), 32)
        wide = x_v[rows, :].astype(F32)
        xg[rows, :] = (wide * gain).astype(BF)
        squares = wide * wide
        total = squares[:, 0:L]
        for j in range(1, 8):
            total = total + squares[:, j * L:(j + 1) * L]
        acc[rows, :] = total
        return carry
    lax.fori_loop(0, 32, scale_rows, 0, unroll=4)

    loads["cot"].wait()
    pl.semaphore_wait(barrier, len(peers))

    for k in range(2):
        go(cores.at[k], corer.at[k], at_core, "core", ("core", k))

    def to_other(first, rows):
        mine = cotf.at[tp, pl.ds(first, rows)]
        go(mine, mine, at_zh, "cot", "cot_z")

    to_other(0, 1024)

    def to_near(half, h, d, key):
        mine = cotf.at[half * 4 + y, halves[h]]
        go(mine, mine, near_dev[d], "cot", key)

    def to_far(half, d, key):
        part = cotf.at[block_of(half, (3, 1)[d]), halves[d]]
        go(part, part, near_dev[d], "cot", key)

    for d in range(2):
        to_near(zh, d, d, "first")
    store_row(sqs, to_row(acc[...]))
    for d in (1, 2, 3):
        go(sqs, sqr.at[d - 1], at_y(d), "sq_y", "sq_y")
    loads["w"].wait()

    def weights(target):
        first = pl.ds(pl.multiple_of(((1 - zh) * 4 + target) * L, L), L)
        second = pl.ds(pl.multiple_of((zh * 4 + target) * L, L), L)
        return jnp.concatenate([w_v[:, first], w_v[:, second]], axis=1)

    def project(rows, cols):
        return jnp.dot(xg[rows, :], cols, preferred_element_type=F32)

    def send_far(d, q):
        go(pf.at[q, halves[d]], ar.at[d, q], near_dev[d], "proj", ("far", q))

    def send_near(d, q):
        go(pn.at[d, q, halves[1 - d]], cr.at[d, q], near_dev[d], "proj", ("near", q))

    def send_onward(q):
        arrived(("far", q), pf.at[q])
        for d in range(2):
            pn[d, q, halves[d], :] = (
                pn[d, q, halves[d], :].astype(F32) + ar[d, q].astype(F32)
            ).astype(BF)
            go(pn.at[d, q, halves[d]], br.at[d, q], near_dev[d], "proj", ("near", q))

    def add_own(k):
        arrived(("core", k), corer.at[k])
        for d in offsets:
            xi = (xx + d) % 4

            def add_partner(zi, carry, k=k, xi=xi):
                both = decoded(zi * 8 + xi * 2 + c, k) + corer[k, xi, zi].astype(F32)
                xs[k, xi, zi] = both.astype(BF)
                return carry
            lax.fori_loop(0, 4, add_partner, 0, unroll=4)
            if d:
                go(xs.at[k, xi], xr.at[k, d - 1], at_x(d), "x", ("x", k))

    cols = weights((y + 2) % 4)
    for d in range(2):
        value = project(halves[d], cols)
        for q in range(2):
            pf[q, halves[d], :] = value[:, q * L:(q + 1) * L].astype(BF)
        send_far(d, 0)
    add_own(0)
    for d in range(2):
        cols = weights((y + (1, 3)[d]) % 4)
        for h in (1 - d, d):
            value = project(halves[h], cols)
            for q in range(2):
                pn[d, q, halves[h], :] = value[:, q * L:(q + 1) * L].astype(BF)
            if h == 1 - d:
                send_near(d, 0)
    add_own(1)

    cols = weights(y)
    for h in range(2):
        value = project(halves[h], cols)
        for q in range(2):
            pown[q, halves[h], :] = value[:, q * L:(q + 1) * L]

    send_onward(0)
    for d in range(2):
        send_far(d, 1)
    for d in range(2):
        send_near(d, 1)

    arrived("sq_y", sqr)
    sqz[...] = sqs[...] + sqr[0] + sqr[1] + sqr[2]
    go(sqz, sqzr, at_zh, "sq_z", "sq_z")

    def along_x(k):
        arrived(("x", k), xr.at[k])

        def add(zi, carry, k=k):
            total = xs[k, xx, zi].astype(F32)
            for s in range(3):
                total = total + xr[k, s, zi].astype(F32)
            zs[k, zi] = total.astype(BF)
            return carry
        lax.fori_loop(0, 4, add, 0, unroll=4)
        for d in (2, 1, 3):
            go(zs.at[k, (zl + d) % 4], zr.at[k, d - 1], at_z(d), "z", ("z", k))

    def outer(k):
        arrived(("z", k), zr.at[k])
        total = zs[k, zl].astype(F32)
        for s in range(3):
            total = total + zr[k, s].astype(F32)
        delta = total * (1.0 / 32.0)
        part = columns_of(k)
        new_momentum = outer_push * mom_v[:, part] + delta
        new_global = glob_v[:, part] - outer_rate * (delta + outer_push * new_momentum)
        nm[:, part] = new_momentum
        ng[:, part] = new_global
        sh[k, c, xx, zl] = new_global.astype(BF)
        here = sh.at[k, c, xx, zl]
        for d in (2, 1, 3):
            go(here, here, at_z(d), "z_back", ("z_back", k))

    def spread_x(k):
        arrived(("z_back", k), zr.at[k])
        here = sh.at[k, c, xx]
        for d in (2, 1, 3):
            go(here, here, at_x(d), "x_back", ("x_back", k))

    def spread_core(k):
        arrived(("x_back", k), xr.at[k])
        go(sh.at[k, c], sh.at[k, c], at_core, "core_back", ("core_back", k))

    def transpose_part(j):
        xgt[pl.ds(j * 256, 256), :] = jnp.transpose(xg[:, pl.ds(j * 256, 256)])

    def send_proj(first, rows):
        part = zsend.at[pl.ds(first, rows)]
        go(part, zrecv.at[pl.ds(first, rows)], at_zh, "proj_z", "proj_z")

    def gather_part(q):
        arrived(("near", q), pf)
        for h in range(2):
            total = pown[q, halves[h], :] + br[h, q].astype(F32) + cr[1 - h, q].astype(F32)
            pown[q, halves[h], :] = total
            if q == 0:
                zsend[halves[h], :] = total.astype(BF)

    def weight_grad(blocks):
        for block in blocks:
            csf[block] = (cotf[block].astype(F32) * invb[...]).astype(BF)
        for i in range(0, len(blocks), 2):
            some = blocks[i:i + 2]
            right = jnp.concatenate([csf[block] for block in some], axis=1)
            value = jnp.dot(xgt[...], right, preferred_element_type=F32)
            for at, block in enumerate(some):
                gw[block] = value[:, at * L:(at + 1) * L]

    def normed_part(blocks, j):
        left = jnp.concatenate([cotf[block] for block in blocks], axis=1)
        rows = pl.ds(pl.multiple_of(j * 256, 256), 256)
        right = jnp.concatenate(
            [w_v[rows, pl.ds(pl.multiple_of(block * L, L), L)] for block in blocks], axis=1
        )
        return lax.dot_general(left, right, (((1,), (1,)), ((), ())), preferred_element_type=F32)

    def normed_grad(blocks, add):
        def keep_part(j, carry):
            value = normed_part(blocks, j)
            gn[j] = gn[j] + value if add else value
            return carry
        lax.fori_loop(0, 4, keep_part, 0)

    def finish_w(k):
        half = half_of(k)

        def block(b, carry):
            rows = pl.ds(pl.multiple_of(b * 32, 32), 32)
            part = columns_of(k)
            step = jnp.concatenate([gw[half * 4 + j, rows, :] for j in range(4)], axis=1)
            mixed = (
                keep_share * w_v[rows, part].astype(F32)
                + (1.0 - keep_share) * sh[k, b % 2, (b // 2) % 4, b // 8].astype(F32)
                - (inner_rate * FACTOR) * step
            )
            nl[rows, part] = mixed.astype(BF)
            return carry
        lax.fori_loop(0, 32, block, 0, unroll=4)

    for j in range(4):
        transpose_part(j)
    normed_grad([tp], False)
    along_x(0)

    gather_part(0)
    send_proj(64, 64)

    send_onward(1)
    for d in range(2):
        to_near(zh, 1 - d, d, "rest")

    along_x(1)
    loads["glob"].wait()
    loads["mom"].wait()
    outer(0)
    send_proj(0, 64)

    arrived("sq_z", sqzr)
    squares = row_of(sqz) + row_of(sqzr)
    inverse = lax.rsqrt(squares * (1.0 / D) + epsilon)
    invb[...] = to_column(inverse)
    arrived("cot_z", cotf.at[other])
    acc[...] = pown[0] * cotf[other].astype(F32)
    weight_grad([tp, other])

    outer(1)
    send_proj(128, 256)

    gather_part(1)
    acc[...] = acc[...] + pown[1] * cotf[tp].astype(F32)
    store_row(ins, to_row(acc[...]))
    for d in (1, 2, 3):
        go(ins, inr.at[d - 1], at_y(d), "in_y", "in_y")

    arrived("first", cotf.at[0])
    for d in range(2):
        to_far(zh, d, "rest")
    for d in range(2):
        to_near(1 - zh, d, d, "other_first")
    for d in range(2):
        to_near(1 - zh, 1 - d, d, "other_rest")

    spread_x(0)

    arrived("in_y", inr)
    inz[...] = ins[...] + inr[0] + inr[1] + inr[2]
    go(inz, inzr, at_zh, "in_z", "in_z")
    send_proj(384, 640)

    spread_x(1)

    arrived("rest", cotf.at[pl.ds(0, 2)])
    near_blocks = [block_of(zh, d) for d in (1, 3)]
    normed_grad([other] + near_blocks + [block_of(zh, 2)], True)

    arrived("other_first", cotf.at[0])
    for d in range(2):
        to_far(1 - zh, d, "other_rest")

    weight_grad(near_blocks)
    spread_core(0)

    arrived("in_z", inzr)
    inner = row_of(inz) + row_of(inzr)
    coefb[...] = to_column(inverse * inverse * inverse * inner * (FACTOR / D))
    arrived("other_rest", cotf.at[pl.ds(0, 2)])
    near_blocks = [block_of(1 - zh, d) for d in (1, 3)]
    last = near_blocks + [block_of(1 - zh, 2)]

    def finish_x(j, carry):
        part = pl.ds(pl.multiple_of(j * 256, 256), 256)
        value = (gn[j] + normed_part(last, j)) * (gain_v[:, part] * FACTOR)
        scale = jnp.concatenate([invb[...]] * 2, axis=1)
        coef = jnp.concatenate([coefb[...]] * 2, axis=1)
        gx[:, part] = (value * scale - x_v[:, part].astype(F32) * coef).astype(BF)
        return carry
    lax.fori_loop(0, 4, finish_x, 0)

    weight_grad([block_of(zh, 2), block_of(1 - zh, 2)])
    weight_grad(near_blocks)
    spread_core(1)
    arrived("proj_z", zrecv)
    proj[...] = ((pown[1] + zrecv[...].astype(F32)) * invb[...] * FACTOR).astype(BF)
    arrived(("core_back", 0), corer.at[0])
    finish_w(0)
    arrived(("core_back", 1), corer.at[1])
    finish_w(1)

    departed("cot", cotf.at[pl.ds(0, 7)])
    departed("proj", cotf.at[pl.ds(0, 6)])
    departed("proj_z", zsend)
    departed("x", xr)
    departed("z", zr)
    departed("z_back", zr)
    departed("x_back", xr)
    departed("core", cores)
    departed("core_back", cores)
    departed("sq_y", sqr)
    departed("in_y", inr)
    departed("sq_z", sqz)
    departed("in_z", inz)
    assert max(len(used) for used in slots.values()) <= SEMS


def writer(*refs):
    sources, targets, sem = refs[:5], refs[5:10], refs[10]
    copies = [pltpu.make_async_copy(s, t, sem.at[i]) for i, (s, t) in enumerate(zip(sources, targets))]
    for copy in copies:
        copy.start()
    for copy in copies:
        copy.wait()


def local(
    tokens_in, gain, cotangent, local_weight, packed_codes, code_scales, global_weight, momentum
):
    any_ = pl.BlockSpec(memory_space=pltpu.HBM)
    vm = pltpu.VMEM
    shapes = (((T, L), BF), ((T, F), BF), ((F, C), BF), ((32, C), F32), ((32, C), F32))
    results = pl.pallas_call(
        kernel,
        out_shape=tuple(vm(*shape) for shape in shapes),
        in_specs=[any_] * 8,
        out_specs=[pl.BlockSpec(memory_space=vm)] * 5,
        scratch_shapes=[
            vm((T, F), BF), vm((1, F), F32), vm((F, C), BF), vm((F, C // 2), jnp.int32), vm((8, F), F32), vm((2, F, 4), F32),
            vm((32, C), F32), vm((32, C), F32),
            vm((T, F), BF), vm((F, T), BF), vm((8, T, L), BF), vm((8, T, L), BF),
            vm((2, T, L), BF), vm((2, 2, T, L), BF), vm((2, T, L), F32),
            vm((2, 2, H, L), BF), vm((2, 2, H, L), BF), vm((2, 2, H, L), BF),
            vm((T, L), BF), vm((T, L), BF),
            vm((2, 4, 4, 32, H), BF), vm((2, 4, 4, 32, H), BF), vm((2, 4, 4, 32, H), BF),
            vm((2, 3, 4, 32, H), BF), vm((2, 4, 32, H), BF), vm((2, 3, 32, H), BF), vm((8, L), F32),
            vm((2, 2, 4, 4, 32, H), BF),
            vm((T, L), F32), vm((T, L), F32), vm((T, L), F32),
            vm((8, L), F32), vm((3, 8, L), F32), vm((8, L), F32), vm((8, L), F32),
            vm((8, L), F32), vm((3, 8, L), F32), vm((8, L), F32), vm((8, L), F32),
            vm((4, T, 256), F32), vm((8, F, L), F32),
            pltpu.SemaphoreType.DMA((SEMS,)), pltpu.SemaphoreType.DMA((SEMS,)),
            pltpu.SemaphoreType.DMA((8,)),
        ],
        compiler_params=pltpu.CompilerParams(
            collective_id=0, has_side_effects=True, vmem_limit_bytes=48 * 2**20
        ),
        cost_estimate=pl.CostEstimate(flops=6 * 2**30, bytes_accessed=12 * 2**20, transcendentals=0),
    )(*(
        pltpu.with_memory_space_constraint(arg, pltpu.HBM) for arg in (
            tokens_in, gain.reshape(1, F), cotangent, local_weight[0], packed_codes[0], code_scales[0].T,
            global_weight[0], momentum[0],
        )
    ))
    projected, grad_x, new_local, new_global, new_momentum = pl.pallas_call(
        writer,
        out_shape=tuple(jax.ShapeDtypeStruct(*shape) for shape in shapes),
        in_specs=[pl.BlockSpec(memory_space=vm)] * 5,
        out_specs=[any_] * 5,
        scratch_shapes=[pltpu.SemaphoreType.DMA((5,))],
        compiler_params=pltpu.CompilerParams(vmem_limit_bytes=8 * 2**20),
    )(*results)
    return (projected, grad_x, new_local[None], new_global[None], new_momentum[None])


def solution(mesh):
    return jax.shard_map(
        local,
        mesh=mesh,
        in_specs=(
            P("rep", "tp"),
            P("tp"),
            P("rep", "tp"),
            P("rep", "tp", None),
            P("rep", "tp", None),
            P("rep", "tp", None),
            P("tp", "rep", None),
            P("tp", "rep", None),
        ),
        out_specs=(
            P("rep", "tp"),
            P("rep", "tp"),
            P("rep", "tp", None),
            P("tp", "rep", None),
            P("tp", "rep", None),
        ),
        check_vma=False,
    )
```

time: 365 us -> 59.9 us (0.16)
  waiting for transfers between devices: 273 us -> 0 us
  Pallas kernels: 0 us -> 58.1 us
  blocking collectives: 22.8 us -> 0 us
  local copies, waits for them, and re-layouts: 20 us -> 0 us
  matrix products: 18.8 us -> 0 us
  between operations: 15.7 us -> 0.64 us
  other arithmetic: 13.9 us -> 0 us
    all_gather x2 -> x0, waiting for transfers between devices: 116 us -> none  [the longest x1 58.5 us: local(): lax.all_gather(shared, 'rep', axis=0, tiled=True).astype(jnp.float32)]
    unnamed x5 -> x0, waiting for transfers between devices: 95.6 us -> none
    reduce_scatter x1 -> x0, waiting for transfers between devices: 61.3 us -> none  [local(): lax.psum_scatter(decode(words, scales).astype(jnp.bfloat16), 'rep', scatt...]
    pallas_call x0 -> x2, Pallas kernels: none -> 58.1 us  [the longest x1 55.9 us: local(): pl.pallas_call(kernel, out_shape=tuple((vm(*shape) for shape in shapes)),...]
    psum x1 -> x0, blocking collectives: 22.8 us -> none  [local(): squares = lax.psum(jnp.sum(wide * wide, axis=-1), 'tp')]
    dot_general x3 -> x0, matrix products: 18.8 us -> none  [the longest x1 6.73 us: local(): lax.dot_general(normed, piece, (((0,), (0,)), ((), ())), preferred_elemen...]
    unnamed x11 -> x0, local copies, waits for them, and re-layouts: 14.5 us -> none
    convert_element_type x2 -> x0, other arithmetic: 8.8 us -> none  [the longest x1 4.56 us: local(): (inverse * scaled - wide * inverse ** 3 * inner / D).astype(jnp.bfloat16)]
  transfers between devices with their start and end apart: 4 -> 0, of which waited for: 4 -> 0; matrix products, arithmetic and copies ran while one was open for 13% -> 0% of each run, Pallas kernels for 0% -> 0%
where the time goes in v2:
time: 59.9 us; the launch traced here: 58.8 us
  Pallas kernels  58.1 us (97%)
  between operations  0.64 us (1%)
    pallas_call x1, Pallas kernels, local(): pl.pallas_call(kernel, out_shape=tuple((vm(*shape) for shape in shapes)),...  55.9 us
    pallas_call x1, Pallas kernels, local(): pl.pallas_call(writer, out_shape=tuple((jax.ShapeDtypeStruct(*shape) for...  2.21 us

profile of v2, /device:TPU:1, one launch (start us, length us, event | category | flops | bytes accessed | tf_op | source)
XLA Modules:
  0.0 58.8 jit_solution(5406563837538719623)
XLA Ops:
  0.6 55.9 %shard_map.119 = (bf16[1024,128]{1,0:T(8,128)(2,1)S(1)}, bf16[1024,1024]{1,0:T(8,128)(2,1)S(1)}, bf16[1024,1024]{1,0:T(8,128)(2,1)S(1)}, f32[32,1024]{1,0:T(8,128)S(1)}, f32[32,1024]{1,0:T(8,128)S(1)}) custom-call(bf16[1024,1024]{1,0:T(8,128)(2,1)} %x_hbm.1, f32[1,1024]{1,0:T(1,128)} %bitcast.19, bf16[1024,128]{1,0:T(8,128)(2,1)} %cot_hbm.1, ...), custom_call_target="tpu_custom_call" | custom-call | flops 6442450944 | bytes 12582912 | tf_op jit(solution)/shard_map/pallas_call | solution.py:475
  56.6 2.2 %shard_map.120 = (bf16[1024,128]{1,0:T(8,128)(2,1)}, bf16[1024,1024]{1,0:T(8,128)(2,1)}, bf16[1024,1024]{1,0:T(8,128)(2,1)}, f32[32,1024]{1,0:T(8,128)}, f32[32,1024]{1,0:T(8,128)}) custom-call(bf16[1024,128]{1,0:T(8,128)(2,1)S(1)} %get-tuple-element.15.refs_0_, bf16[1024,1024]{1,0:T(8,128)(2,1)S(1)} %get-tuple-element.16.refs_1_, ...), custom_call_target="tpu_custom_call" | custom-call | tf_op jit(solution)/shard_map/pallas_call | solution.py:507

commit v3 on v2

--- a/solution.py
+++ b/solution.py
@@ -16,6 +16,8 @@
 F = 1024
 C = 1024
 H = 512
+Q = 256
+PARTS = 4
 L = 128
 FACTOR = 1.0 / math.sqrt(D)
 
@@ -111,19 +113,20 @@
     for dev in peers:
         pl.semaphore_signal(barrier, inc=1, device_id=dev, device_id_type=MESH)
 
-    def half_of(k):
-        return zh if k == 0 else 1 - zh
+    def half_of(m):
+        return zh if m == 0 else 1 - zh
 
     def columns_of(k):
-        return pl.ds(pl.multiple_of(half_of(k) * H, H), H)
+        return pl.ds(pl.multiple_of(half_of(k // 2) * H + (k % 2) * Q, Q), Q)
 
     def decoded(block, k):
         rows = pl.ds(pl.multiple_of(block * 32, 32), 32)
-        words = codes_v[rows, :]
-        codes = (jnp.bitwise_and(jnp.right_shift(words, 4 * half_of(k)), 15) - 8).astype(F32)
-        scales = scales_v[k, rows, :]
+        words = codes_v[rows, pl.ds((k % 2) * Q, Q)]
+        codes = (jnp.bitwise_and(jnp.right_shift(words, 4 * half_of(k // 2)), 15) - 8).astype(F32)
+        scales = scales_v[k // 2, rows, :]
         return jnp.concatenate(
-            [codes[:, g * L:(g + 1) * L] * scales[:, g:g + 1] for g in range(4)], axis=1
+            [codes[:, g * L:(g + 1) * L] * scales[:, (k % 2) * 2 + g:(k % 2) * 2 + g + 1] for g in range(2)],
+            axis=1,
         )
 
     offsets = (2, 1, 3, 0)
@@ -140,7 +143,7 @@
     scales_v[0] = jnp.where(zh == 0, first, second)
     scales_v[1] = jnp.where(zh == 0, second, first)
     loads["codes"].wait()
-    for k in range(2):
+    for k in range(PARTS):
         def for_partner(i, carry, k=k):
             cores[k, i // 4, i % 4] = decoded((i % 4) * 8 + (i // 4) * 2 + (1 - c), k).astype(BF)
             return carry
@@ -165,14 +168,14 @@
     loads["cot"].wait()
     pl.semaphore_wait(barrier, len(peers))
 
-    for k in range(2):
+    for k in range(PARTS):
         go(cores.at[k], corer.at[k], at_core, "core", ("core", k))
 
     def to_other(first, rows):
         mine = cotf.at[tp, pl.ds(first, rows)]
         go(mine, mine, at_zh, "cot", "cot_z")
 
-    to_other(0, 1024)
+    to_other(0, 512)
 
     def to_near(half, h, d, key):
         mine = cotf.at[half * 4 + y, halves[h]]
@@ -231,6 +234,7 @@
             pf[q, halves[d], :] = value[:, q * L:(q + 1) * L].astype(BF)
         send_far(d, 0)
     add_own(0)
+    add_own(1)
     for d in range(2):
         cols = weights((y + (1, 3)[d]) % 4)
         for h in (1 - d, d):
@@ -239,7 +243,8 @@
                 pn[d, q, halves[h], :] = value[:, q * L:(q + 1) * L].astype(BF)
             if h == 1 - d:
                 send_near(d, 0)
-    add_own(1)
+    add_own(2)
+    add_own(3)
 
     cols = weights(y)
     for h in range(2):
@@ -336,91 +341,106 @@
             return carry
         lax.fori_loop(0, 4, keep_part, 0)
 
-    def finish_w(k):
-        half = half_of(k)
+    def finish_w(m):
+        half = half_of(m)
 
         def block(b, carry):
             rows = pl.ds(pl.multiple_of(b * 32, 32), 32)
-            part = columns_of(k)
+            part = pl.ds(pl.multiple_of(half * H, H), H)
             step = jnp.concatenate([gw[half * 4 + j, rows, :] for j in range(4)], axis=1)
+            shared = jnp.concatenate([sh[2 * m + i, b % 2, (b // 2) % 4, b // 8] for i in range(2)], axis=1)
             mixed = (
                 keep_share * w_v[rows, part].astype(F32)
-                + (1.0 - keep_share) * sh[k, b % 2, (b // 2) % 4, b // 8].astype(F32)
+                + (1.0 - keep_share) * shared.astype(F32)
                 - (inner_rate * FACTOR) * step
             )
             nl[rows, part] = mixed.astype(BF)
             return carry
         lax.fori_loop(0, 32, block, 0, unroll=4)
 
+    along_x(0)
+    to_other(512, 256)
     for j in range(4):
         transpose_part(j)
+    along_x(1)
+    to_other(768, 256)
     normed_grad([tp], False)
-    along_x(0)
-
-    gather_part(0)
-    send_proj(64, 64)
-
-    send_onward(1)
-    for d in range(2):
-        to_near(zh, 1 - d, d, "rest")
-
-    along_x(1)
     loads["glob"].wait()
     loads["mom"].wait()
     outer(0)
-    send_proj(0, 64)
+    along_x(2)
+
+    gather_part(0)
+    outer(1)
+
+    send_onward(1)
+    for d in range(2):
+        to_near(zh, 1 - d, d, "rest")
+    arrived("first", cotf.at[0])
+    for d in range(2):
+        to_far(zh, d, "rest")
+
+    along_x(3)
+    spread_x(0)
+    outer(2)
 
     arrived("sq_z", sqzr)
     squares = row_of(sqz) + row_of(sqzr)
     inverse = lax.rsqrt(squares * (1.0 / D) + epsilon)
     invb[...] = to_column(inverse)
+    spread_x(1)
     arrived("cot_z", cotf.at[other])
     acc[...] = pown[0] * cotf[other].astype(F32)
     weight_grad([tp, other])
 
-    outer(1)
-    send_proj(128, 256)
+    outer(3)
+    send_proj(0, 256)
 
     gather_part(1)
     acc[...] = acc[...] + pown[1] * cotf[tp].astype(F32)
     store_row(ins, to_row(acc[...]))
     for d in (1, 2, 3):
         go(ins, inr.at[d - 1], at_y(d), "in_y", "in_y")
-
-    arrived("first", cotf.at[0])
-    for d in range(2):
-        to_far(zh, d, "rest")
     for d in range(2):
         to_near(1 - zh, d, d, "other_first")
     for d in range(2):
-        to_near(1 - zh, 1 - d, d, "other_rest")
-
-    spread_x(0)
-
+        to_near(1 - zh, 1 - d, d, "other_second")
+
+    spread_x(2)
+    spread_core(0)
+
+    spread_x(3)
+    send_proj(256, 256)
+    spread_core(1)
+
+    arrived("rest", cotf.at[pl.ds(0, 2)])
+    near_blocks = [block_of(zh, d) for d in (1, 3)]
+    normed_grad([other] + near_blocks + [block_of(zh, 2)], True)
+
+    arrived("other_first", cotf.at[0])
+    for d in range(2):
+        to_far(1 - zh, d, "other_far")
     arrived("in_y", inr)
     inz[...] = ins[...] + inr[0] + inr[1] + inr[2]
     go(inz, inzr, at_zh, "in_z", "in_z")
-    send_proj(384, 640)
-
-    spread_x(1)
-
-    arrived("rest", cotf.at[pl.ds(0, 2)])
-    near_blocks = [block_of(zh, d) for d in (1, 3)]
-    normed_grad([other] + near_blocks + [block_of(zh, 2)], True)
-
-    arrived("other_first", cotf.at[0])
-    for d in range(2):
-        to_far(1 - zh, d, "other_rest")
-
-    weight_grad(near_blocks)
-    spread_core(0)
-
+    send_proj(512, 512)
+
+    spread_core(2)
+    weight_grad(near_blocks + [block_of(zh, 2)])
+    spread_core(3)
+    for k in (0, 1):
+        arrived(("core_back", k), corer.at[k])
+    finish_w(0)
+
+    arrived("other_second", cotf.at[0])
+    near_blocks = [block_of(1 - zh, d) for d in (1, 3)]
+    normed_grad(near_blocks, True)
     arrived("in_z", inzr)
     inner = row_of(inz) + row_of(inzr)
     coefb[...] = to_column(inverse * inverse * inverse * inner * (FACTOR / D))
-    arrived("other_rest", cotf.at[pl.ds(0, 2)])
-    near_blocks = [block_of(1 - zh, d) for d in (1, 3)]
-    last = near_blocks + [block_of(1 - zh, 2)]
+    weight_grad(near_blocks)
+    arrived("other_far", cotf.at[0])
+    last = [block_of(1 - zh, 2)]
 
     def finish_x(j, carry):
         part = pl.ds(pl.multiple_of(j * 256, 256), 256)
@@ -431,14 +451,11 @@
         return carry
     lax.fori_loop(0, 4, finish_x, 0)
 
-    weight_grad([block_of(zh, 2), block_of(1 - zh, 2)])
-    weight_grad(near_blocks)
-    spread_core(1)
+    weight_grad(last)
     arrived("proj_z", zrecv)
     proj[...] = ((pown[1] + zrecv[...].astype(F32)) * invb[...] * FACTOR).astype(BF)
-    arrived(("core_back", 0), corer.at[0])
-    finish_w(0)
-    arrived(("core_back", 1), corer.at[1])
+    for k in (2, 3):
+        arrived(("core_back", k), corer.at[k])
     finish_w(1)
 
     departed("cot", cotf.at[pl.ds(0, 7)])
@@ -484,9 +501,9 @@
             vm((2, T, L), BF), vm((2, 2, T, L), BF), vm((2, T, L), F32),
             vm((2, 2, H, L), BF), vm((2, 2, H, L), BF), vm((2, 2, H, L), BF),
             vm((T, L), BF), vm((T, L), BF),
-            vm((2, 4, 4, 32, H), BF), vm((2, 4, 4, 32, H), BF), vm((2, 4, 4, 32, H), BF),
-            vm((2, 3, 4, 32, H), BF), vm((2, 4, 32, H), BF), vm((2, 3, 32, H), BF), vm((8, L), F32),
-            vm((2, 2, 4, 4, 32, H), BF),
+            vm((PARTS, 4, 4, 32, Q), BF), vm((PARTS, 4, 4, 32, Q), BF), vm((PARTS, 4, 4, 32, Q), BF),
+            vm((PARTS, 3, 4, 32, Q), BF), vm((PARTS, 4, 32, Q), BF), vm((PARTS, 3, 32, Q), BF), vm((8, L), F32),
+            vm((PARTS, 2, 4, 4, 32, Q), BF),
             vm((T, L), F32), vm((T, L), F32), vm((T, L), F32),
             vm((8, L), F32), vm((3, 8, L), F32), vm((8, L), F32), vm((8, L), F32),
             vm((8, L), F32), vm((3, 8, L), F32), vm((8, L), F32), vm((8, L), F32),

time: 59.9 us -> 57.3 us (0.957)
  the two profiles are of different devices: /device:TPU:1 before, /device:TPU:46 now
where the time goes in v3:
time: 57.3 us; the launch traced here: 57.2 us
  Pallas kernels  56.6 us (99%)
  between operations  0.64 us (1%)
    pallas_call x1, Pallas kernels, local(): pl.pallas_call(kernel, out_shape=tuple((vm(*shape) for shape in shapes)),...  54.4 us
    pallas_call x1, Pallas kernels, local(): pl.pallas_call(writer, out_shape=tuple((jax.ShapeDtypeStruct(*shape) for...  2.21 us

profile of v3, /device:TPU:46, one launch (start us, length us, event | category | flops | bytes accessed | tf_op | source)
XLA Modules:
  0.0 57.2 jit_solution(2044390981409734717)
XLA Ops:
  0.6 54.4 %shard_map.119 = (bf16[1024,128]{1,0:T(8,128)(2,1)S(1)}, bf16[1024,1024]{1,0:T(8,128)(2,1)S(1)}, bf16[1024,1024]{1,0:T(8,128)(2,1)S(1)}, f32[32,1024]{1,0:T(8,128)S(1)}, f32[32,1024]{1,0:T(8,128)S(1)}) custom-call(bf16[1024,1024]{1,0:T(8,128)(2,1)} %x_hbm.1, f32[1,1024]{1,0:T(1,128)} %bitcast.19, bf16[1024,128]{1,0:T(8,128)(2,1)} %cot_hbm.1, ...), custom_call_target="tpu_custom_call" | custom-call | flops 6442450944 | bytes 12582912 | tf_op jit(solution)/shard_map/pallas_call | solution.py:492
  55.0 2.2 %shard_map.120 = (bf16[1024,128]{1,0:T(8,128)(2,1)}, bf16[1024,1024]{1,0:T(8,128)(2,1)}, bf16[1024,1024]{1,0:T(8,128)(2,1)}, f32[32,1024]{1,0:T(8,128)}, f32[32,1024]{1,0:T(8,128)}) custom-call(bf16[1024,128]{1,0:T(8,128)(2,1)S(1)} %get-tuple-element.15.refs_0_, bf16[1024,1024]{1,0:T(8,128)(2,1)S(1)} %get-tuple-element.16.refs_1_, ...), custom_call_target="tpu_custom_call" | custom-call | tf_op jit(solution)/shard_map/pallas_call | solution.py:524

commit v4 on v3

--- a/solution.py
+++ b/solution.py
@@ -394,7 +394,7 @@
     weight_grad([tp, other])
 
     outer(3)
-    send_proj(0, 256)
+    send_proj(0, 128)
 
     gather_part(1)
     acc[...] = acc[...] + pown[1] * cotf[tp].astype(F32)
@@ -410,7 +410,7 @@
     spread_core(0)
 
     spread_x(3)
-    send_proj(256, 256)
+    send_proj(128, 384)
     spread_core(1)
 
     arrived("rest", cotf.at[pl.ds(0, 2)])

time: 57.3 us -> 63.2 us (1.10)
  the two profiles are of different devices: /device:TPU:46 before, /device:TPU:38 now
where the time goes in v4:
time: 63.2 us; the launch traced here: 63.1 us
  Pallas kernels  62.5 us (99%)
  between operations  0.64 us (1%)
    pallas_call x1, Pallas kernels, local(): pl.pallas_call(kernel, out_shape=tuple((vm(*shape) for shape in shapes)),...  60.3 us
    pallas_call x1, Pallas kernels, local(): pl.pallas_call(writer, out_shape=tuple((jax.ShapeDtypeStruct(*shape) for...  2.21 us

profile of v4, /device:TPU:38, one launch (start us, length us, event | category | flops | bytes accessed | tf_op | source)
XLA Modules:
  0.0 63.1 jit_solution(12244751986280639893)
XLA Ops:
  0.6 60.3 %shard_map.119 = (bf16[1024,128]{1,0:T(8,128)(2,1)S(1)}, bf16[1024,1024]{1,0:T(8,128)(2,1)S(1)}, bf16[1024,1024]{1,0:T(8,128)(2,1)S(1)}, f32[32,1024]{1,0:T(8,128)S(1)}, f32[32,1024]{1,0:T(8,128)S(1)}) custom-call(bf16[1024,1024]{1,0:T(8,128)(2,1)} %x_hbm.1, f32[1,1024]{1,0:T(1,128)} %bitcast.19, bf16[1024,128]{1,0:T(8,128)(2,1)} %cot_hbm.1, ...), custom_call_target="tpu_custom_call" | custom-call | flops 6442450944 | bytes 12582912 | tf_op jit(solution)/shard_map/pallas_call | solution.py:492
  60.9 2.2 %shard_map.120 = (bf16[1024,128]{1,0:T(8,128)(2,1)}, bf16[1024,1024]{1,0:T(8,128)(2,1)}, bf16[1024,1024]{1,0:T(8,128)(2,1)}, f32[32,1024]{1,0:T(8,128)}, f32[32,1024]{1,0:T(8,128)}) custom-call(bf16[1024,128]{1,0:T(8,128)(2,1)S(1)} %get-tuple-element.15.refs_0_, bf16[1024,1024]{1,0:T(8,128)(2,1)S(1)} %get-tuple-element.16.refs_1_, ...), custom_call_target="tpu_custom_call" | custom-call | tf_op jit(solution)/shard_map/pallas_call | solution.py:524
